TPU v7x, 512 devices: a whole 4x4x16 slice. The times are simulated.
512 devices in a mesh: ctx: 64 (over z_lo, x, core), head: 8 (over z_hi, y).
Axes of the slice: x: 4, y: 4, z: 16 (z_hi: 2, z_lo: 8; z = z_hi * 8 + z_lo), core: 2. Of those that a mesh axis runs over, the one named last changes fastest.
Arguments:
- queries: bfloat16 [24576, 7168], P('ctx', 'head'), may hold values from -160 to 160
- keys: bfloat16 [24576, 1024], P('ctx', 'head'), may hold values from -6 to 6
- values: bfloat16 [24576, 1024], P('ctx', 'head'), may hold values from -6 to 6
- out_grad: bfloat16 [24576, 7168], P('ctx', 'head'), may hold values from -6 to 6
- outputs: bfloat16 [24576, 7168], P('ctx', 'head'), may hold values from -4 to 4
- block_ids: int32 [128], replicated, may hold values from 0 to 127, each once
Outputs:
- grad_queries: bfloat16 [24576, 7168], P('ctx', 'head')
- grad_keys: bfloat16 [24576, 1024], P('ctx', 'head')
- grad_values: bfloat16 [24576, 1024], P('ctx', 'head')
- grad_square: float32 [], replicated
All inputs are finite; a program needn't handle non-finite values.
Results may differ from a plain program's by a relative error of at most 0.015.
Values may be sent and summed in bfloat16 or wider, within the bound.
A program may use at most 64 MiB of HBM per device.

v0:
```python
import jax
import jax.numpy as jnp
from jax import lax
from jax.sharding import PartitionSpec as P

NEG = -1e30


def from_behind(value, axis, steps):
    count = lax.axis_size(axis)
    pairs = [(source, (source + steps) % count) for source in range(count)]
    return lax.ppermute(value, axis, pairs)


def positions(block_ids, device, tokens_here):
    half = tokens_here // 2
    pair = lax.dynamic_slice(block_ids, (2 * device,), (2,))
    rows = jnp.arange(tokens_here, dtype=jnp.int32)
    return jnp.where(rows < half, pair[0] * half + rows, pair[1] * half + rows - half)


def masked_scores(heads_q, block_k, pos_q, pos_k):
    scale = heads_q.shape[-1] ** (-0.5)
    scores = jnp.einsum("tjd,ud->jtu", heads_q, block_k, preferred_element_type=jnp.float32) * scale
    seen = pos_k[None, :] <= pos_q[:, None]
    return (jnp.where(seen[None], scores, NEG), seen)


def block_stats(heads_q, block_k, pos_q, pos_k):

    def work():
        scores, seen = masked_scores(heads_q, block_k, pos_q, pos_k)
        peak = jnp.max(scores, axis=2)
        total = jnp.sum(jnp.where(seen[None], jnp.exp(scores - peak[:, :, None]), 0.0), axis=2)
        return (peak, total)

    return work()


def block_grads(heads_q, heads_do, lse, delta, block_k, block_v, pos_q, pos_k):
    scale = heads_q.shape[-1] ** (-0.5)

    def work():
        scores, seen = masked_scores(heads_q, block_k, pos_q, pos_k)
        probs = jnp.where(seen[None], jnp.exp(scores - lse[:, :, None]), 0.0)
        probs_low = probs.astype(jnp.bfloat16)
        dprobs = jnp.einsum("tjd,ud->jtu", heads_do, block_v, preferred_element_type=jnp.float32)
        dscore = (probs * (dprobs - delta[:, :, None]) * scale).astype(jnp.bfloat16)
        grad_v = jnp.einsum("jtu,tjd->ud", probs_low, heads_do, preferred_element_type=jnp.float32)
        grad_k = jnp.einsum("jtu,tjd->ud", dscore, heads_q, preferred_element_type=jnp.float32)
        grad_q = jnp.einsum("jtu,ud->tjd", dscore, block_k, preferred_element_type=jnp.float32)
        return (grad_q, grad_k, grad_v)

    return work()


def merged_lse(stat_list):
    peak = stat_list[0][0]
    for entry in stat_list[1:]:
        peak = jnp.maximum(peak, entry[0])
    total = stat_list[0][1] * jnp.exp(stat_list[0][0] - peak)
    for entry in stat_list[1:]:
        total = total + entry[1] * jnp.exp(entry[0] - peak)
    return peak + jnp.log(total)


def keys_move(key_rows, value_rows, by):
    return from_behind((key_rows, value_rows), "ctx", by)


def kgrad_move(part_k, part_v, by):
    return from_behind((part_k, part_v), "ctx", by)


def shards(queries, keys, values, out_grad, outputs, block_ids):
    tokens_here = queries.shape[0]
    head_size = keys.shape[1]
    group = queries.shape[1] // head_size
    cycle_size = lax.axis_size("ctx")
    place = lax.axis_index("ctx")
    pos_me = positions(block_ids, place, tokens_here)
    pos_left = positions(block_ids, (place - 1) % cycle_size, tokens_here)
    pos_right = positions(block_ids, (place + 1) % cycle_size, tokens_here)
    heads_q = queries.reshape(tokens_here, group, head_size)
    heads_do = out_grad.reshape(tokens_here, group, head_size)
    heads_out = outputs.reshape(tokens_here, group, head_size)
    delta = jnp.transpose(
        jnp.sum(heads_do.astype(jnp.float32) * heads_out.astype(jnp.float32), axis=2)
    )
    k_left, v_left = keys_move(keys, values, 1)
    k_right, v_right = keys_move(keys, values, -1)
    own_stats = block_stats(heads_q, keys, pos_me, pos_me)
    left_stats = block_stats(heads_q, k_left, pos_me, pos_left)
    right_stats = block_stats(heads_q, k_right, pos_me, pos_right)
    lse = merged_lse([own_stats, left_stats, right_stats])
    own = block_grads(heads_q, heads_do, lse, delta, keys, values, pos_me, pos_me)
    with_left = block_grads(heads_q, heads_do, lse, delta, k_left, v_left, pos_me, pos_left)
    with_right = block_grads(heads_q, heads_do, lse, delta, k_right, v_right, pos_me, pos_right)
    grad_q = own[0] + with_left[0] + with_right[0]
    back_right = kgrad_move(with_left[1], with_left[2], -1)
    back_left = kgrad_move(with_right[1], with_right[2], 1)
    grad_k = own[1] + back_right[0] + back_left[0]
    grad_v = own[2] + back_right[1] + back_left[1]
    local_square = jnp.sum(grad_q * grad_q) + jnp.sum(grad_k * grad_k) + jnp.sum(grad_v * grad_v)
    total_square = lax.psum(local_square, ("ctx", "head"))
    count = tokens_here * cycle_size * lax.axis_size("head") * (group + 2) * head_size
    grad_square = total_square / count
    grad_queries = grad_q.reshape(tokens_here, group * head_size).astype(jnp.bfloat16)
    return (grad_queries, grad_k.astype(jnp.bfloat16), grad_v.astype(jnp.bfloat16), grad_square)


def solution(mesh):
    return jax.shard_map(
        shards,
        mesh=mesh,
        in_specs=(
            P("ctx", "head"),
            P("ctx", "head"),
            P("ctx", "head"),
            P("ctx", "head"),
            P("ctx", "head"),
            P(),
        ),
        out_specs=(P("ctx", "head"), P("ctx", "head"), P("ctx", "head"), P()),
        check_vma=False,
    )
```

profile of v0, /device:TPU:1, one launch (start us, length us, event | category | flops | bytes accessed | tf_op | source)
XLA Modules:
  0.0 197.0 jit_solution(16411330572361810206)
XLA Ops:
  0.6 8.9 %collective-permute-start.3 = (bf16[384,128]{1,0:T(8,128)(2,1)}, bf16[384,128]{1,0:T(8,128)(2,1)S(1)}, u32[]{:S(2)}, u32[]{:S(2)}) collective-permute-start(bf16[384,128]{1,0:T(8,128)(2,1)} %param.8), channel_id=1, source_target_pairs={{0,504},{8,0},{16,8},{24,16},{32,24},{40,32},{48,40},{56,48},{64,5... | collective-permute-start | bytes 294920 | tf_op jit(solution)/shard_map/ppermute | solution.py:12
  9.6 1.9 collective-permute-start.2
  11.5 1.9 collective-permute-start
  13.4 9.4 %collective-permute-start.1 = (bf16[384,128]{1,0:T(8,128)(2,1)}, bf16[384,128]{1,0:T(8,128)(2,1)S(1)}, u32[]{:S(2)}, u32[]{:S(2)}) collective-permute-start(bf16[384,128]{1,0:T(8,128)(2,1)} %param.7), channel_id=1, source_target_pairs={{0,504},{8,0},{16,8},{24,16},{32,24},{40,32},{48,40},{56,48},{64,5... | collective-permute-start | bytes 294920 | tf_op jit(solution)/shard_map/ppermute | solution.py:12
  22.9 0.8 fusion.65
  28.8 1.5 copy.29
  30.3 1.5 copy.33
  31.7 1.5 copy.35
  33.5 0.8 fusion.12
  34.4 1.0 select_reduce_fusion.2
  35.6 0.8 fusion.14
  36.4 1.0 select_reduce_fusion
  37.4 0.8 fusion.13
  38.2 1.0 select_reduce_fusion.1
  39.3 1.2 fusion.28
  40.5 1.7 fusion.8
  42.3 1.2 fusion.31
  43.5 1.9 fusion.5
  45.4 0.7 convolution_bitcast_fusion.1
  46.1 1.8 fusion.2
  47.9 0.7 convolution_bitcast_fusion
  48.6 1.9 collective-permute-start.5
  50.5 1.9 collective-permute-start.7
  52.5 12.4 %collective-permute-start.4 = (f32[384,128]{1,0:T(8,128)S(1)}, f32[384,128]{1,0:T(8,128)S(1)}, u32[]{:S(2)}, u32[]{:S(2)}) collective-permute-start(f32[384,128]{1,0:T(8,128)S(1)} %convolution_bitcast_fusion.1), channel_id=1, source_target_pairs={{0,504},{8,0},{16,8},{24,16},{32,24},{40,32},{48,40},{56,48},{64,5... | collective-permute-start | bytes 589832 | tf_op jit(solution)/shard_map/ppermute | solution.py:12
  64.8 12.4 %collective-permute-start.6 = (f32[384,128]{1,0:T(8,128)S(1)}, f32[384,128]{1,0:T(8,128)S(1)}, u32[]{:S(2)}, u32[]{:S(2)}) collective-permute-start(f32[384,128]{1,0:T(8,128)S(1)} %fusion.28), channel_id=1, source_target_pairs={{0,504},{8,0},{16,8},{24,16},{32,24},{40,32},{48,40},{56,48},{64,5... | collective-permute-start | bytes 589832 | tf_op jit(solution)/shard_map/ppermute | solution.py:12
  77.2 0.6 fusion.51
  77.8 0.6 convolution_add_fusion.1
  78.4 1.4 multiply_reduce_fusion
  79.8 2.0 multiply_reduce_fusion.2
  83.1 4.5 %multiply_reduce_fusion.1 = (f32[]{:T(128)}, bf16[384,128]{1,0:T(8,128)(2,1)}) fusion(f32[384,128]{1,0:T(8,128)S(1)} %collective-permute-done.7, f32[384,128]{1,0:T(8,128)S(1)} %collective-permute-done.6, bf16[384,7,128]{0,2,1:T(8,128)(2,1)S(1)} %bitcast.169, f32[384,384,7]{1,0,2:T(8,128)} %copy-done, f32[7,384]{1,0:T(8,128)S(1)} %log_add_fusion, ...), kind=kOutput, calls=%fused_computation.51 | convolution fusion | flops 269647872 | bytes 5466628 | tf_op jit(solution)/shard_map/jtu,tjd->ud/dot_general | solution.py:49
  88.2 1.1 copy.50
  89.4 105.8 %psum.7 = f32[]{:T(128)} all-reduce(f32[]{:T(128)S(6)} %add.184), channel_id=1, replica_groups=mesh['ctx'=64,'head'=8] {'ctx','head'}, use_global_device_ids=true, to_apply=%region_10.11 | all-reduce | flops 1 | bytes 8 | tf_op jit(solution)/shard_map/psum | solution.py:105
  (22 shorter events, 1.8 us)
Async XLA Ops:
  0.6 32.9 %copy-start.1 = (bf16[384,128]{1,0:T(8,128)(2,1)S(1)}, bf16[384,128]{1,0:T(8,128)(2,1)}, u32[]{:S(2)}) copy-start(bf16[384,128]{1,0:T(8,128)(2,1)} %param.7) | copy-start | bytes 294916
  0.6 45.5 %collective-permute-start.3 = (bf16[384,128]{1,0:T(8,128)(2,1)}, bf16[384,128]{1,0:T(8,128)(2,1)S(1)}, u32[]{:S(2)}, u32[]{:S(2)}) collective-permute-start(bf16[384,128]{1,0:T(8,128)(2,1)} %param.8), channel_id=1, source_target_pairs={{0,504},{8,0},{16,8},{24,16},{32,24},{40,32},{48,40},{56,48},{64,5... | collective-permute-start | bytes 294920 | tf_op jit(solution)/shard_map/ppermute | solution.py:12
  9.6 33.9 %collective-permute-start.2 = (bf16[384,128]{1,0:T(8,128)(2,1)}, bf16[384,128]{1,0:T(8,128)(2,1)S(1)}, u32[]{:S(2)}, u32[]{:S(2)}) collective-permute-start(bf16[384,128]{1,0:T(8,128)(2,1)} %param.8), channel_id=1, source_target_pairs={{0,8},{8,16},{16,24},{24,32},{32,40},{40,48},{48,56},{56,64},{64,7... | collective-permute-start | bytes 294920 | tf_op jit(solution)/shard_map/ppermute | solution.py:12
  11.5 25.9 %collective-permute-start = (bf16[384,128]{1,0:T(8,128)(2,1)}, bf16[384,128]{1,0:T(8,128)(2,1)S(1)}, u32[]{:S(2)}, u32[]{:S(2)}) collective-permute-start(bf16[384,128]{1,0:T(8,128)(2,1)} %param.7), channel_id=1, source_target_pairs={{0,8},{8,16},{16,24},{24,32},{32,40},{40,48},{48,56},{56,64},{64,7... | collective-permute-start | bytes 294920 | tf_op jit(solution)/shard_map/ppermute | solution.py:12
  13.4 22.2 %collective-permute-start.1 = (bf16[384,128]{1,0:T(8,128)(2,1)}, bf16[384,128]{1,0:T(8,128)(2,1)S(1)}, u32[]{:S(2)}, u32[]{:S(2)}) collective-permute-start(bf16[384,128]{1,0:T(8,128)(2,1)} %param.7), channel_id=1, source_target_pairs={{0,504},{8,0},{16,8},{24,16},{32,24},{40,32},{48,40},{56,48},{64,5... | collective-permute-start | bytes 294920 | tf_op jit(solution)/shard_map/ppermute | solution.py:12
  34.4 6.1 %copy-start = (f32[384,384,7]{1,0,2:T(8,128)}, f32[384,384,7]{1,0,2:T(8,128)S(1)}, u32[]{:S(2)}) copy-start(f32[384,384,7]{1,0,2:T(8,128)S(1)} %get-tuple-element.35) | copy-start | bytes 12386308
  39.3 1.2 copy-start.2
  48.6 31.2 %collective-permute-start.5 = (f32[384,128]{1,0:T(8,128)S(1)}, f32[384,128]{1,0:T(8,128)S(1)}, u32[]{:S(2)}, u32[]{:S(2)}) collective-permute-start(f32[384,128]{1,0:T(8,128)S(1)} %convolution_bitcast_fusion), channel_id=1, source_target_pairs={{0,8},{8,16},{16,24},{24,32},{32,40},{40,48},{48,56},{56,64},{64,7... | collective-permute-start | bytes 589832 | tf_op jit(solution)/shard_map/ppermute | solution.py:12
  50.5 32.5 %collective-permute-start.7 = (f32[384,128]{1,0:T(8,128)S(1)}, f32[384,128]{1,0:T(8,128)S(1)}, u32[]{:S(2)}, u32[]{:S(2)}) collective-permute-start(f32[384,128]{1,0:T(8,128)S(1)} %fusion.31), channel_id=1, source_target_pairs={{0,8},{8,16},{16,24},{24,32},{32,40},{40,48},{48,56},{56,64},{64,7... | collective-permute-start | bytes 589832 | tf_op jit(solution)/shard_map/ppermute | solution.py:12
  52.5 27.3 %collective-permute-start.4 = (f32[384,128]{1,0:T(8,128)S(1)}, f32[384,128]{1,0:T(8,128)S(1)}, u32[]{:S(2)}, u32[]{:S(2)}) collective-permute-start(f32[384,128]{1,0:T(8,128)S(1)} %convolution_bitcast_fusion.1), channel_id=1, source_target_pairs={{0,504},{8,0},{16,8},{24,16},{32,24},{40,32},{48,40},{56,48},{64,5... | collective-permute-start | bytes 589832 | tf_op jit(solution)/shard_map/ppermute | solution.py:12
  64.8 18.2 %collective-permute-start.6 = (f32[384,128]{1,0:T(8,128)S(1)}, f32[384,128]{1,0:T(8,128)S(1)}, u32[]{:S(2)}, u32[]{:S(2)}) collective-permute-start(f32[384,128]{1,0:T(8,128)S(1)} %fusion.28), channel_id=1, source_target_pairs={{0,504},{8,0},{16,8},{24,16},{32,24},{40,32},{48,40},{56,48},{64,5... | collective-permute-start | bytes 589832 | tf_op jit(solution)/shard_map/ppermute | solution.py:12
where the time goes:
time: 198 us; the launch traced here: 197 us
  blocking collectives  106 us (54%)
  starting transfers between devices  50.7 us (26%)
  matrix products  20.7 us (10%)
  between operations  8.6 us (4%)
  local copies, waits for them, and re-layouts  7.53 us (4%)
  other arithmetic  3.57 us (2%)
    psum x1, blocking collectives, shards(): total_square = lax.psum(local_square, ('ctx', 'head'))  106 us
    ppermute x8, starting transfers between devices, from_behind(): return lax.ppermute(value, axis, pairs)  50.7 us
    dot_general x3, matrix products, work(): jnp.einsum('jtu,tjd->ud', probs_low, heads_do, preferred_element_type=jnp...  6.89 us
    unnamed x10, local copies, waits for them, and re-layouts  5.51 us
    dot_general x3, matrix products, work(): jnp.einsum('tjd,ud->jtu', heads_do, block_v, preferred_element_type=jnp.f...  5.44 us
  transfers between devices with their start and end apart: 8, of which 0 were waited for; matrix products, arithmetic and copies ran while one was open for 12% of the time, Pallas kernels for 0%

commit v1 on v0

v1 whole, which is shorter than its diff:
```python
import jax
import jax.numpy as jnp
from jax import lax
from jax.experimental import pallas as pl
from jax.experimental.pallas import tpu as pltpu
from jax.sharding import PartitionSpec as P

HD = 128
GROUP = 7
TOK = 384
BLK = 192
N_CTX = 64
SCALE = HD**-0.5
EXP2_SCALE = SCALE * 1.4426950408889634
NEG = -1e30
BIG = 1e30
HEAD_SETS = ((0, 1), (2, 3), (4, 5), (6,))
OWN, NEAR, FAR = 0, 1, 2
MESH = pl.DeviceIdType.MESH
f32 = jnp.float32
bf16 = jnp.bfloat16


def dot_nt(a, b):
    return lax.dot_general(a, b, (((1,), (1,)), ((), ())), preferred_element_type=f32)


def dot_nn(a, b):
    return lax.dot_general(a, b, (((1,), (0,)), ((), ())), preferred_element_type=f32)


def fold(x):
    rows, cols = x.shape
    y = jnp.sum(x.reshape(rows // 8, 8, cols), axis=0)
    out = y[:, :128]
    for c in range(128, cols, 128):
        out = out + y[:, c : c + 128]
    return out


def kernel(
    q_hbm, k_hbm, v_hbm, do_hbm, o_hbm, ids,
    gq_hbm, gk_hbm, gv_hbm, sq_out,
    q, do, o, kv, s, dpd, p, ds, delta, mask, acc, gq, gkv,
    part, back, red, red_src,
    load_sem, out_sem, kv_send, kv_recv, part_send, part_recv, red_send, red_recv,
):
    me = lax.axis_index("ctx")
    hd = lax.axis_index("head")
    core = lax.rem(me, 2)
    near = me + 1 - 2 * core
    far = lax.rem(me + N_CTX - 1 + 2 * core, N_CTX)
    plane = me // 8
    spot = lax.rem(me, 8)
    others = {NEAR: near, FAR: far}

    partners = [[], [], []]
    for j in range(1, 8):
        partners[0].append({"ctx": plane * 8 + lax.rem(spot + j, 8), "head": hd})
        partners[1].append({"ctx": me, "head": lax.rem(hd + j, 8)})
        partners[2].append({"ctx": lax.rem(plane + j, 8) * 8 + spot, "head": hd})

    loads = [
        pltpu.make_async_copy(src, dst, load_sem.at[i])
        for i, (src, dst) in enumerate(
            [(q_hbm, q), (k_hbm, kv.at[0, OWN]), (v_hbm, kv.at[1, OWN]), (do_hbm, do), (o_hbm, o)]
        )
    ]
    for c in loads:
        c.start()
    barrier = pltpu.get_barrier_semaphore()
    greet = [{"ctx": near, "head": hd}, {"ctx": far, "head": hd}] + sum(partners, [])
    for dev in greet:
        pl.semaphore_signal(barrier, inc=1, device_id=dev, device_id_type=MESH)
    pl.semaphore_wait(barrier, len(greet))

    sends = {}
    for i, src in ((0, k_hbm), (1, v_hbm)):
        for side in (FAR, NEAR):
            c = pltpu.make_async_remote_copy(
                src_ref=src,
                dst_ref=kv.at[i, side],
                send_sem=kv_send.at[i, side],
                recv_sem=kv_recv.at[i, side],
                device_id={"ctx": others[side], "head": hd},
                device_id_type=MESH,
            )
            c.start()
            sends[i, side] = c

    lane = lax.broadcasted_iota(jnp.int32, (1, TOK), 1)
    row = lax.broadcasted_iota(jnp.int32, (TOK, 1), 0)
    id0, id1 = ids[2 * me], ids[2 * me + 1]
    qid = jnp.where(lane < BLK, id0, id1)
    pos_q = qid * BLK + jnp.where(lane < BLK, lane, lane - BLK)
    pos_k = jnp.where(row < BLK, id0 * BLK + row, id1 * BLK + row - BLK)
    mask[...] = jnp.where(pos_k <= pos_q, 0.0, NEG).astype(f32)
    seen = {
        side: [jnp.where(ids[2 * others[side] + b] < qid, 1, 0) for b in (0, 1)]
        for side in (NEAR, FAR)
    }

    for c in loads:
        c.wait()

    cols = lax.broadcasted_iota(jnp.int32, (TOK, HD), 1)
    gather = jnp.zeros((TOK, HD), f32)
    for h in range(GROUP):
        c = slice(h * HD, (h + 1) * HD)
        d = jnp.sum(do[:, c].astype(f32) * o[:, c].astype(f32), axis=1, keepdims=True)
        gather = jnp.where(cols == h, d, gather)
    delta[...] = gather.T[:8]

    def stack(ref, hs):
        return jnp.concatenate([ref[:, h * HD : (h + 1) * HD] for h in hs], axis=0)

    def rep(x, n):
        return jnp.concatenate([x] * n, axis=1)

    def span(hs):
        return slice(hs[0] * TOK, (hs[-1] + 1) * TOK)

    def rows(side):
        return slice(side * TOK, (side + 1) * TOK)

    peaks = {}

    def scores(side, hs):
        x = dot_nt(kv[0, side], stack(q, hs))
        if side == OWN:
            x = x + rep(mask[...], len(hs))
            peaks[side, hs] = [jnp.max(x, axis=0, keepdims=True)]
        else:
            peaks[side, hs] = [
                jnp.max(x[b * BLK : (b + 1) * BLK], axis=0, keepdims=True) for b in (0, 1)
            ]
        s[rows(side), span(hs)] = x

    def dprobs(side, hs):
        row_delta = jnp.concatenate([delta[h : h + 1] for h in hs], axis=1)
        return (dot_nt(kv[1, side], stack(do, hs)) - row_delta).astype(bf16)

    for hs in HEAD_SETS:
        scores(OWN, hs)
        dpd[rows(OWN), span(hs)] = dprobs(OWN, hs)
    sends[0, NEAR].wait_recv()
    sends[1, NEAR].wait_recv()
    for hs in HEAD_SETS:
        scores(NEAR, hs)
        dpd[rows(NEAR), span(hs)] = dprobs(NEAR, hs)
    sends[0, FAR].wait_recv()
    sends[1, FAR].wait_recv()

    norm = {}
    scaled = {}

    def softmax(hs):
        n = len(hs)
        m = peaks[OWN, hs][0]
        vis = {}
        for side in (NEAR, FAR):
            for b in (0, 1):
                vis[side, b] = rep(seen[side][b], n) > 0
                m = jnp.maximum(m, jnp.where(vis[side, b], peaks[side, hs][b], NEG))
        e = jnp.exp2((s[rows(OWN), span(hs)] - m) * EXP2_SCALE)
        total = jnp.sum(e, axis=0, keepdims=True)
        p[rows(OWN), span(hs)] = e.astype(bf16)
        for side in (NEAR, FAR):
            for b in (0, 1):
                r = slice(side * TOK + b * BLK, side * TOK + (b + 1) * BLK)
                shift = jnp.where(vis[side, b], m, BIG)
                e = jnp.exp2((s[r, span(hs)] - shift) * EXP2_SCALE)
                total = total + jnp.sum(e, axis=0, keepdims=True)
                p[r, span(hs)] = e.astype(bf16)
        inv = 1.0 / total
        norm[hs] = inv * SCALE
        cols_inv = jnp.concatenate(
            [
                jnp.broadcast_to(inv[:, i * TOK : (i + 1) * TOK], (HD, TOK)).T
                for i in range(n)
            ],
            axis=0,
        )
        scaled[hs] = (
            (stack(q, hs).astype(f32) * (cols_inv * SCALE)).astype(bf16),
            (stack(do, hs).astype(f32) * cols_inv).astype(bf16),
        )

    def key_grads(side, hs, first):
        r, c = rows(side), span(hs)
        qn, don = scaled[hs]
        if side == FAR:
            d = dprobs(FAR, hs)
        else:
            d = dpd[r, c]
        w = p[r, c]
        dsv = d * w
        ds[r, c] = dsv
        gk = dot_nn(dsv, qn)
        gv = dot_nn(w, don)
        if first:
            acc[0, side], acc[1, side] = gk, gv
        else:
            acc[0, side] += gk
            acc[1, side] += gv

    def send_back(side):
        out = []
        for i in (0, 1):
            part[i, side - 1] = acc[i, side].astype(bf16)
            c = pltpu.make_async_remote_copy(
                src_ref=part.at[i, side - 1],
                dst_ref=back.at[i, side - 1],
                send_sem=part_send.at[i, side - 1],
                recv_sem=part_recv.at[i, side - 1],
                device_id={"ctx": others[side], "head": hd},
                device_id_type=MESH,
            )
            c.start()
            out.append(c)
        return out

    scores(FAR, HEAD_SETS[0])
    for n, hs in enumerate(HEAD_SETS):
        if n + 1 < len(HEAD_SETS):
            scores(FAR, HEAD_SETS[n + 1])
        softmax(hs)
        key_grads(FAR, hs, n == 0)
    returns = {FAR: send_back(FAR)}
    for n, hs in enumerate(HEAD_SETS):
        key_grads(NEAR, hs, n == 0)
    returns[NEAR] = send_back(NEAR)
    for n, hs in enumerate(HEAD_SETS):
        key_grads(OWN, hs, n == 0)

    square = jnp.zeros((8, 128), f32)
    k_t = kv[0].reshape(3 * TOK, HD).T
    for hs in HEAD_SETS:
        g = dot_nn(k_t, ds[:, span(hs)]) * norm[hs]
        square = square + fold(g * g)
        for i, h in enumerate(hs):
            gq[:, h * HD : (h + 1) * HD] = g[:, i * TOK : (i + 1) * TOK].T.astype(bf16)
    outs = [pltpu.make_async_copy(gq, gq_hbm, out_sem.at[0])]
    outs[0].start()

    for side in (NEAR, FAR):
        for c in returns[side]:
            c.wait_recv()
    for i, dst in ((0, gk_hbm), (1, gv_hbm)):
        g = acc[i, OWN] + back[i, 0].astype(f32) + back[i, 1].astype(f32)
        square = square + fold(g * g)
        gkv[i] = g.astype(bf16)
        c = pltpu.make_async_copy(gkv.at[i], dst, out_sem.at[1 + i])
        c.start()
        outs.append(c)

    sent = []
    for r, place in enumerate((spot, hd, plane)):
        red_src[r] = square
        red[r, place] = square
        copies = []
        for j in range(1, 8):
            c = pltpu.make_async_remote_copy(
                src_ref=red_src.at[r],
                dst_ref=red.at[r, place],
                send_sem=red_send.at[r, j],
                recv_sem=red_recv.at[r, j],
                device_id=partners[r][j - 1],
                device_id_type=MESH,
            )
            c.start()
            copies.append(c)
        for c in copies:
            c.wait_recv()
        sent += copies
        square = red[r, 0]
        for j in range(1, 8):
            square = square + red[r, j]
    count = TOK * N_CTX * 8 * (GROUP + 2) * HD
    sq_out[0, 0] = jnp.sum(square) / count

    for c in sent + list(sends.values()) + returns[NEAR] + returns[FAR]:
        c.wait_send()
    for c in outs:
        c.wait()


def shards(queries, keys, values, out_grad, outputs, block_ids):
    hbm = pl.BlockSpec(memory_space=pl.ANY)
    smem = pl.BlockSpec(memory_space=pltpu.SMEM)
    wide = GROUP * TOK
    dma = pltpu.SemaphoreType.DMA
    gq, gk, gv, square = pl.pallas_call(
        kernel,
        out_shape=(
            jax.ShapeDtypeStruct((TOK, GROUP * HD), bf16),
            jax.ShapeDtypeStruct((TOK, HD), bf16),
            jax.ShapeDtypeStruct((TOK, HD), bf16),
            jax.ShapeDtypeStruct((1, 1), f32),
        ),
        in_specs=[hbm] * 5 + [smem],
        out_specs=(hbm, hbm, hbm, smem),
        scratch_shapes=[
            pltpu.VMEM((TOK, GROUP * HD), bf16),
            pltpu.VMEM((TOK, GROUP * HD), bf16),
            pltpu.VMEM((TOK, GROUP * HD), bf16),
            pltpu.VMEM((2, 3, TOK, HD), bf16),
            pltpu.VMEM((3 * TOK, wide), f32),
            pltpu.VMEM((2 * TOK, wide), bf16),
            pltpu.VMEM((3 * TOK, wide), bf16),
            pltpu.VMEM((3 * TOK, wide), bf16),
            pltpu.VMEM((8, TOK), f32),
            pltpu.VMEM((TOK, TOK), f32),
            pltpu.VMEM((2, 3, TOK, HD), f32),
            pltpu.VMEM((TOK, GROUP * HD), bf16),
            pltpu.VMEM((2, TOK, HD), bf16),
            pltpu.VMEM((2, 2, TOK, HD), bf16),
            pltpu.VMEM((2, 2, TOK, HD), bf16),
            pltpu.VMEM((3, 8, 8, 128), f32),
            pltpu.VMEM((3, 8, 128), f32),
            dma((5,)),
            dma((3,)),
            dma((2, 3)),
            dma((2, 3)),
            dma((2, 2)),
            dma((2, 2)),
            dma((3, 8)),
            dma((3, 8)),
        ],
        compiler_params=pltpu.CompilerParams(
            collective_id=0, has_side_effects=True, vmem_limit_bytes=56 * 2**20
        ),
        name="grads",
    )(queries, keys, values, out_grad, outputs, block_ids)
    return gq, gk, gv, square.reshape(())


def solution(mesh):
    return jax.shard_map(
        shards,
        mesh=mesh,
        in_specs=(
            P("ctx", "head"),
            P("ctx", "head"),
            P("ctx", "head"),
            P("ctx", "head"),
            P("ctx", "head"),
            P(),
        ),
        out_specs=(P("ctx", "head"), P("ctx", "head"), P("ctx", "head"), P()),
        check_vma=False,
    )
```

time: 198 us -> 63 us (0.32)
  blocking collectives: 106 us -> 0 us
  Pallas kernels: 0 us -> 56.7 us
  starting transfers between devices: 50.7 us -> 0 us
  matrix products: 20.7 us -> 0 us
  between operations: 8.6 us -> 2.45 us
  local copies, waits for them, and re-layouts: 7.53 us -> 3.61 us
  other arithmetic: 3.57 us -> 0 us
    psum x1 -> x0, blocking collectives: 106 us -> none  [shards(): total_square = lax.psum(local_square, ('ctx', 'head'))]
    pallas_call x0 -> x1, Pallas kernels: none -> 56.7 us  [shards(): pl.pallas_call(kernel, out_shape=(jax.ShapeDtypeStruct((TOK, GROUP * HD),...]
    ppermute x8 -> x0, starting transfers between devices: 50.7 us -> none  [from_behind(): return lax.ppermute(value, axis, pairs)]
    dot_general x15 -> x0, matrix products: 20.7 us -> none  [the longest x3 6.89 us: work(): jnp.einsum('jtu,tjd->ud', probs_low, heads_do, preferred_element_type=jnp...]
    reduce_sum x4 -> x0, other arithmetic: 3.21 us -> none  [the longest x3 3.01 us: work(): jnp.sum(jnp.where(seen[None], jnp.exp(scores - peak[:, :, None]), 0.0), a...]
    unnamed x10 -> x7, local copies, waits for them, and re-layouts: 5.51 us -> 3.61 us
  transfers between devices with their start and end apart: 8 -> 0, of which waited for: 0 -> 0; matrix products, arithmetic and copies ran while one was open for 12% -> 0% of each run, Pallas kernels for 0% -> 0%
where the time goes in v1:
time: 63 us; the launch traced here: 62.7 us
  Pallas kernels  56.7 us (90%)
  local copies, waits for them, and re-layouts  3.61 us (6%)
  between operations  2.45 us (4%)
    pallas_call x1, Pallas kernels, shards(): pl.pallas_call(kernel, out_shape=(jax.ShapeDtypeStruct((TOK, GROUP * HD),...  56.7 us
    unnamed x7, local copies, waits for them, and re-layouts  3.61 us

profile of v1, /device:TPU:1, one launch (start us, length us, event | category | flops | bytes accessed | tf_op | source)
XLA Modules:
  0.0 62.7 jit_solution(11029287006065529647)
XLA Ops:
  0.6 56.7 %grads.1 = (bf16[384,896]{1,0:T(8,128)(2,1)}, bf16[384,128]{1,0:T(8,128)(2,1)}, bf16[384,128]{1,0:T(8,128)(2,1)}, f32[1,1]{1,0:T(1,128)}) custom-call(bf16[384,896]{1,0:T(8,128)(2,1)} %q_hbm.1, bf16[384,128]{1,0:T(8,128)(2,1)} %k_hbm.1, bf16[384,128]{1,0:T(8,128)(2,1)} %v_hbm.1, bf16[384,896]{1,0:T(8,128)(2,1)} %do_hbm.1, bf16[384,896]{1,0:T(8,128)(2,1)} %o_hbm.1, ...), custom_call_target="tpu_custom_call" | custom-call | tf_op jit(solution)/shard_map/grads/pallas_call | solution.py:293
  57.3 0.0 copy-start.1
  57.3 2.0 %copy.14 = bf16[384,896]{1,0:T(8,128)(2,1)} copy(bf16[384,896]{1,0:T(8,128)(2,1)} %get-tuple-element.16) | data formatting | bytes 1376256
  59.4 0.0 copy-done.1
  59.4 0.0 copy-start
  59.4 0.6 %copy.15 = bf16[384,128]{1,0:T(8,128)(2,1)} copy(bf16[384,128]{1,0:T(8,128)(2,1)S(1)} %copy-done.1) | data formatting | bytes 196608
  60.0 0.3 copy-done
  60.3 0.6 %copy.16 = bf16[384,128]{1,0:T(8,128)(2,1)} copy(bf16[384,128]{1,0:T(8,128)(2,1)S(1)} %copy-done) | data formatting | bytes 196608
Async XLA Ops:
  57.3 2.0 %copy-start.1 = (bf16[384,128]{1,0:T(8,128)(2,1)S(1)}, bf16[384,128]{1,0:T(8,128)(2,1)}, u32[]{:S(2)}) copy-start(bf16[384,128]{1,0:T(8,128)(2,1)} %get-tuple-element.17) | copy-start | bytes 294916
  59.4 0.9 %copy-start = (bf16[384,128]{1,0:T(8,128)(2,1)S(1)}, bf16[384,128]{1,0:T(8,128)(2,1)}, u32[]{:S(2)}) copy-start(bf16[384,128]{1,0:T(8,128)(2,1)} %get-tuple-element.18) | copy-start | bytes 294916

commit v2 on v1

--- a/solution.py
+++ b/solution.py
@@ -42,7 +42,7 @@
     q_hbm, k_hbm, v_hbm, do_hbm, o_hbm, ids,
     gq_hbm, gk_hbm, gv_hbm, sq_out,
     q, do, o, kv, s, dpd, p, ds, delta, mask, acc, gq, gkv,
-    part, back, red, red_src,
+    part, back, red_a, red_b, red_src,
     load_sem, out_sem, kv_send, kv_recv, part_send, part_recv, red_send, red_recv,
 ):
     me = lax.axis_index("ctx")
@@ -54,12 +54,22 @@
     spot = lax.rem(me, 8)
     others = {NEAR: near, FAR: far}
 
-    partners = [[], [], []]
-    for j in range(1, 8):
-        partners[0].append({"ctx": plane * 8 + lax.rem(spot + j, 8), "head": hd})
-        partners[1].append({"ctx": me, "head": lax.rem(hd + j, 8)})
-        partners[2].append({"ctx": lax.rem(plane + j, 8) * 8 + spot, "head": hd})
-
+    y = lax.rem(hd, 4)
+    deep = (hd // 4) * 8 + plane
+
+    def across(j):
+        return {"ctx": plane * 8 + lax.rem(spot + j % 8, 8), "head": hd - y + lax.rem(y + j // 8, 4)}
+
+    def along(j):
+        z = lax.rem(deep + j, 16)
+        return {"ctx": lax.rem(z, 8) * 8 + spot, "head": (z // 8) * 4 + y}
+
+    partners = [[across(j) for j in range(1, 32)], [along(j) for j in range(1, 16)]]
+
+    barrier = pltpu.get_barrier_semaphore()
+    greet = [{"ctx": far, "head": hd}, {"ctx": near, "head": hd}] + partners[0] + partners[1]
+    for dev in greet:
+        pl.semaphore_signal(barrier, inc=1, device_id=dev, device_id_type=MESH)
     loads = [
         pltpu.make_async_copy(src, dst, load_sem.at[i])
         for i, (src, dst) in enumerate(
@@ -68,10 +78,6 @@
     ]
     for c in loads:
         c.start()
-    barrier = pltpu.get_barrier_semaphore()
-    greet = [{"ctx": near, "head": hd}, {"ctx": far, "head": hd}] + sum(partners, [])
-    for dev in greet:
-        pl.semaphore_signal(barrier, inc=1, device_id=dev, device_id_type=MESH)
     pl.semaphore_wait(barrier, len(greet))
 
     sends = {}
@@ -240,6 +246,7 @@
         square = square + fold(g * g)
         for i, h in enumerate(hs):
             gq[:, h * HD : (h + 1) * HD] = g[:, i * TOK : (i + 1) * TOK].T.astype(bf16)
+
     outs = [pltpu.make_async_copy(gq, gq_hbm, out_sem.at[0])]
     outs[0].start()
 
@@ -255,17 +262,18 @@
         outs.append(c)
 
     sent = []
-    for r, place in enumerate((spot, hd, plane)):
-        red_src[r] = square
-        red[r, place] = square
+    value = jnp.sum(square, axis=0, keepdims=True)
+    for r, (place, slots) in enumerate(((y * 8 + spot, red_a), (deep, red_b))):
+        red_src[r] = value
+        slots[place] = value
         copies = []
-        for j in range(1, 8):
+        for j, dev in enumerate(partners[r]):
             c = pltpu.make_async_remote_copy(
                 src_ref=red_src.at[r],
-                dst_ref=red.at[r, place],
+                dst_ref=slots.at[place],
                 send_sem=red_send.at[r, j],
                 recv_sem=red_recv.at[r, j],
-                device_id=partners[r][j - 1],
+                device_id=dev,
                 device_id_type=MESH,
             )
             c.start()
@@ -273,15 +281,32 @@
         for c in copies:
             c.wait_recv()
         sent += copies
-        square = red[r, 0]
-        for j in range(1, 8):
-            square = square + red[r, j]
+        value = jnp.sum(slots[...], axis=0)
     count = TOK * N_CTX * 8 * (GROUP + 2) * HD
-    sq_out[0, 0] = jnp.sum(square) / count
+    sq_out[0, 0] = jnp.sum(value) / count
 
     for c in sent + list(sends.values()) + returns[NEAR] + returns[FAR]:
         c.wait_send()
     for c in outs:
+        c.wait()
+
+
+def place_outputs(gq, gk, gv, gq_out, gk_out, gv_out, wide, narrow, sem_in, sem_out):
+    parts = []
+    for i, (src, dst) in enumerate(((gk, gk_out), (gv, gv_out))):
+        parts.append((src, narrow.at[i], dst))
+    step = TOK // 4
+    for i in range(4):
+        r = pl.ds(i * step, step)
+        parts.append((gq.at[r], wide.at[r], gq_out.at[r]))
+    first = [pltpu.make_async_copy(a, b, sem_in.at[n]) for n, (a, b, _) in enumerate(parts)]
+    second = [pltpu.make_async_copy(b, c, sem_out.at[n]) for n, (_, b, c) in enumerate(parts)]
+    for c in first:
+        c.start()
+    for a, b in zip(first, second):
+        a.wait()
+        b.start()
+    for c in second:
         c.wait()
 
 
@@ -316,22 +341,36 @@
             pltpu.VMEM((2, TOK, HD), bf16),
             pltpu.VMEM((2, 2, TOK, HD), bf16),
             pltpu.VMEM((2, 2, TOK, HD), bf16),
-            pltpu.VMEM((3, 8, 8, 128), f32),
-            pltpu.VMEM((3, 8, 128), f32),
+            pltpu.VMEM((32, 1, 128), f32),
+            pltpu.VMEM((16, 1, 128), f32),
+            pltpu.VMEM((2, 1, 128), f32),
             dma((5,)),
             dma((3,)),
             dma((2, 3)),
             dma((2, 3)),
             dma((2, 2)),
             dma((2, 2)),
-            dma((3, 8)),
-            dma((3, 8)),
+            dma((2, 31)),
+            dma((2, 31)),
         ],
         compiler_params=pltpu.CompilerParams(
             collective_id=0, has_side_effects=True, vmem_limit_bytes=56 * 2**20
         ),
         name="grads",
     )(queries, keys, values, out_grad, outputs, block_ids)
+    gq, gk, gv = pl.pallas_call(
+        place_outputs,
+        out_shape=tuple(jax.ShapeDtypeStruct(x.shape, x.dtype) for x in (gq, gk, gv)),
+        in_specs=[hbm] * 3,
+        out_specs=(hbm,) * 3,
+        scratch_shapes=[
+            pltpu.VMEM((TOK, GROUP * HD), bf16),
+            pltpu.VMEM((2, TOK, HD), bf16),
+            dma((6,)),
+            dma((6,)),
+        ],
+        name="place_outputs",
+    )(gq, gk, gv)
     return gq, gk, gv, square.reshape(())
 
 

time: 63 us -> 56.1 us (0.89)
  local copies, waits for them, and re-layouts: 3.61 us -> 0 us
  Pallas kernels: 56.7 us -> 53.5 us
    pallas_call x1, Pallas kernels: 56.7 us -> 51.5 us  [shards(): pl.pallas_call(kernel, out_shape=(jax.ShapeDtypeStruct((TOK, GROUP * HD),...]
    unnamed x7 -> x0, local copies, waits for them, and re-layouts: 3.61 us -> none
    pallas_call x0 -> x1, Pallas kernels: none -> 2.01 us  [shards(): pl.pallas_call(place_outputs, out_shape=tuple((jax.ShapeDtypeStruct(x.sha...]
where the time goes in v2:
time: 56.1 us; the launch traced here: 55.9 us
  Pallas kernels  53.5 us (95%)
  between operations  2.38 us (4%)
    pallas_call x1, Pallas kernels, shards(): pl.pallas_call(kernel, out_shape=(jax.ShapeDtypeStruct((TOK, GROUP * HD),...  51.5 us
    pallas_call x1, Pallas kernels, shards(): pl.pallas_call(place_outputs, out_shape=tuple((jax.ShapeDtypeStruct(x.sha...  2.01 us

profile of v2, /device:TPU:1, one launch (start us, length us, event | category | flops | bytes accessed | tf_op | source)
XLA Modules:
  0.0 55.9 jit_solution(5236374178578468435)
XLA Ops:
  0.6 51.5 %grads.1 = (bf16[384,896]{1,0:T(8,128)(2,1)}, bf16[384,128]{1,0:T(8,128)(2,1)}, bf16[384,128]{1,0:T(8,128)(2,1)}, f32[1,1]{1,0:T(1,128)}) custom-call(bf16[384,896]{1,0:T(8,128)(2,1)} %q_hbm.1, bf16[384,128]{1,0:T(8,128)(2,1)} %k_hbm.1, bf16[384,128]{1,0:T(8,128)(2,1)} %v_hbm.1, bf16[384,896]{1,0:T(8,128)(2,1)} %do_hbm.1, bf16[384,896]{1,0:T(8,128)(2,1)} %o_hbm.1, ...), custom_call_target="tpu_custom_call" | custom-call | tf_op jit(solution)/shard_map/grads/pallas_call | solution.py:318
  52.2 2.0 %place_outputs.1 = (bf16[384,896]{1,0:T(8,128)(2,1)}, bf16[384,128]{1,0:T(8,128)(2,1)}, bf16[384,128]{1,0:T(8,128)(2,1)}) custom-call(bf16[384,896]{1,0:T(8,128)(2,1)} %get-tuple-element.11.gq, bf16[384,128]{1,0:T(8,128)(2,1)} %get-tuple-element.12.gk, bf16[384,128]{1,0:T(8,128)(2,1)} %get-tuple-element.13.gv), custom_call_target="tpu_custom_call" | custom-call | tf_op jit(solution)/shard_map/place_outputs/pallas_call | solution.py:361

commit v3 on v2

--- a/solution.py
+++ b/solution.py
@@ -41,7 +41,7 @@
 def kernel(
     q_hbm, k_hbm, v_hbm, do_hbm, o_hbm, ids,
     gq_hbm, gk_hbm, gv_hbm, sq_out,
-    q, do, o, kv, s, dpd, p, ds, delta, mask, acc, gq, gkv,
+    q, do, o, kv, s, dpd, p, ds, delta, mask, acc, gq_t, gq, gkv,
     part, back, red_a, red_b, red_src,
     load_sem, out_sem, kv_send, kv_recv, part_send, part_recv, red_send, red_recv,
 ):
@@ -146,113 +146,135 @@
         row_delta = jnp.concatenate([delta[h : h + 1] for h in hs], axis=1)
         return (dot_nt(kv[1, side], stack(do, hs)) - row_delta).astype(bf16)
 
+    def visible(side, b, hs):
+        return rep(seen[side][b], len(hs)) > 0
+
+    def masked_probs(side, hs, m, total):
+        for b in (0, 1):
+            r = slice(side * TOK + b * BLK, side * TOK + (b + 1) * BLK)
+            shift = jnp.where(visible(side, b, hs), m, BIG)
+            e = jnp.exp2((s[r, span(hs)] - shift) * EXP2_SCALE)
+            total = total + jnp.sum(e, axis=0, keepdims=True)
+            p[r, span(hs)] = e.astype(bf16)
+        return total
+
+    def raised(side, hs, m):
+        for b in (0, 1):
+            m = jnp.maximum(m, jnp.where(visible(side, b, hs), peaks[side, hs][b], NEG))
+        return m
+
+    def columns(row, n):
+        return jnp.concatenate(
+            [jnp.broadcast_to(row[:, i * TOK : (i + 1) * TOK], (HD, TOK)).T for i in range(n)],
+            axis=0,
+        )
+
+    def scaled(ref, hs, cols, factor):
+        return (stack(ref, hs).astype(f32) * (cols * factor)).astype(bf16)
+
+    first_stats, stats, far_scale = {}, {}, {}
+
+    def near_part(hs):
+        m = raised(NEAR, hs, peaks[OWN, hs][0])
+        e = jnp.exp2((s[rows(OWN), span(hs)] - m) * EXP2_SCALE)
+        total = jnp.sum(e, axis=0, keepdims=True)
+        w = e.astype(bf16)
+        p[rows(OWN), span(hs)] = w
+        ds[rows(OWN), span(hs)] = dpd[:, span(hs)] * w
+        total = masked_probs(NEAR, hs, m, total)
+        ds[rows(NEAR), span(hs)] = dprobs(NEAR, hs) * p[rows(NEAR), span(hs)]
+        first_stats[hs] = (m, total)
+
+    def far_values(hs, first):
+        m1, total1 = first_stats[hs]
+        m = raised(FAR, hs, m1)
+        f = jnp.exp2((m1 - m) * EXP2_SCALE)
+        total = masked_probs(FAR, hs, m, total1 * f)
+        inv = 1.0 / total
+        stats[hs] = (f, inv)
+        cols = columns(inv, len(hs))
+        far_scale[hs] = cols
+        add(1, FAR, first, dot_nn(p[rows(FAR), span(hs)], scaled(do, hs, cols, 1.0)))
+
+    def add(i, side, first, x):
+        if first:
+            acc[i, side] = x
+        else:
+            acc[i, side] += x
+
+    def far_keys(hs, first):
+        d = dprobs(FAR, hs) * p[rows(FAR), span(hs)]
+        ds[rows(FAR), span(hs)] = d
+        add(0, FAR, first, dot_nn(d, scaled(q, hs, far_scale[hs], SCALE)))
+
+    def send_back(side, i):
+        part[i, side - 1] = acc[i, side].astype(bf16)
+        c = pltpu.make_async_remote_copy(
+            src_ref=part.at[i, side - 1],
+            dst_ref=back.at[i, side - 1],
+            send_sem=part_send.at[i, side - 1],
+            recv_sem=part_recv.at[i, side - 1],
+            device_id={"ctx": others[side], "head": hd},
+            device_id_type=MESH,
+        )
+        c.start()
+        return c
+
+    last = len(HEAD_SETS) - 1
+
     for hs in HEAD_SETS:
         scores(OWN, hs)
-        dpd[rows(OWN), span(hs)] = dprobs(OWN, hs)
+        dpd[:, span(hs)] = dprobs(OWN, hs)
     sends[0, NEAR].wait_recv()
     sends[1, NEAR].wait_recv()
-    for hs in HEAD_SETS:
-        scores(NEAR, hs)
-        dpd[rows(NEAR), span(hs)] = dprobs(NEAR, hs)
+    scores(NEAR, HEAD_SETS[0])
+    k_t = kv[0, 0:2].reshape(2 * TOK, HD).T
+    for n, hs in enumerate(HEAD_SETS):
+        if n < last:
+            scores(NEAR, HEAD_SETS[n + 1])
+        near_part(hs)
+        gq_t[:, span(hs)] = dot_nn(k_t, ds[: 2 * TOK, span(hs)])
+
     sends[0, FAR].wait_recv()
-    sends[1, FAR].wait_recv()
-
-    norm = {}
-    scaled = {}
-
-    def softmax(hs):
-        n = len(hs)
-        m = peaks[OWN, hs][0]
-        vis = {}
-        for side in (NEAR, FAR):
-            for b in (0, 1):
-                vis[side, b] = rep(seen[side][b], n) > 0
-                m = jnp.maximum(m, jnp.where(vis[side, b], peaks[side, hs][b], NEG))
-        e = jnp.exp2((s[rows(OWN), span(hs)] - m) * EXP2_SCALE)
-        total = jnp.sum(e, axis=0, keepdims=True)
-        p[rows(OWN), span(hs)] = e.astype(bf16)
-        for side in (NEAR, FAR):
-            for b in (0, 1):
-                r = slice(side * TOK + b * BLK, side * TOK + (b + 1) * BLK)
-                shift = jnp.where(vis[side, b], m, BIG)
-                e = jnp.exp2((s[r, span(hs)] - shift) * EXP2_SCALE)
-                total = total + jnp.sum(e, axis=0, keepdims=True)
-                p[r, span(hs)] = e.astype(bf16)
-        inv = 1.0 / total
-        norm[hs] = inv * SCALE
-        cols_inv = jnp.concatenate(
-            [
-                jnp.broadcast_to(inv[:, i * TOK : (i + 1) * TOK], (HD, TOK)).T
-                for i in range(n)
-            ],
-            axis=0,
-        )
-        scaled[hs] = (
-            (stack(q, hs).astype(f32) * (cols_inv * SCALE)).astype(bf16),
-            (stack(do, hs).astype(f32) * cols_inv).astype(bf16),
-        )
-
-    def key_grads(side, hs, first):
-        r, c = rows(side), span(hs)
-        qn, don = scaled[hs]
-        if side == FAR:
-            d = dprobs(FAR, hs)
-        else:
-            d = dpd[r, c]
-        w = p[r, c]
-        dsv = d * w
-        ds[r, c] = dsv
-        gk = dot_nn(dsv, qn)
-        gv = dot_nn(w, don)
-        if first:
-            acc[0, side], acc[1, side] = gk, gv
-        else:
-            acc[0, side] += gk
-            acc[1, side] += gv
-
-    def send_back(side):
-        out = []
-        for i in (0, 1):
-            part[i, side - 1] = acc[i, side].astype(bf16)
-            c = pltpu.make_async_remote_copy(
-                src_ref=part.at[i, side - 1],
-                dst_ref=back.at[i, side - 1],
-                send_sem=part_send.at[i, side - 1],
-                recv_sem=part_recv.at[i, side - 1],
-                device_id={"ctx": others[side], "head": hd},
-                device_id_type=MESH,
-            )
-            c.start()
-            out.append(c)
-        return out
-
     scores(FAR, HEAD_SETS[0])
     for n, hs in enumerate(HEAD_SETS):
-        if n + 1 < len(HEAD_SETS):
+        if n < last:
             scores(FAR, HEAD_SETS[n + 1])
-        softmax(hs)
-        key_grads(FAR, hs, n == 0)
-    returns = {FAR: send_back(FAR)}
+        far_values(hs, n == 0)
+    returns = [send_back(FAR, 1)]
+    sends[1, FAR].wait_recv()
     for n, hs in enumerate(HEAD_SETS):
-        key_grads(NEAR, hs, n == 0)
-    returns[NEAR] = send_back(NEAR)
+        far_keys(hs, n == 0)
+    returns.append(send_back(FAR, 0))
+
+    near_scale = {}
     for n, hs in enumerate(HEAD_SETS):
-        key_grads(OWN, hs, n == 0)
+        f, inv = stats[hs]
+        cols = columns(f * inv, len(hs))
+        near_scale[hs] = (scaled(q, hs, cols, SCALE), scaled(do, hs, cols, 1.0))
+        qn, don = near_scale[hs]
+        add(1, NEAR, n == 0, dot_nn(p[rows(NEAR), span(hs)], don))
+        add(0, NEAR, n == 0, dot_nn(ds[rows(NEAR), span(hs)], qn))
+    returns += [send_back(NEAR, 1), send_back(NEAR, 0)]
+    for n, hs in enumerate(HEAD_SETS):
+        qn, don = near_scale[hs]
+        add(1, OWN, n == 0, dot_nn(p[rows(OWN), span(hs)], don))
+        add(0, OWN, n == 0, dot_nn(ds[rows(OWN), span(hs)], qn))
 
     square = jnp.zeros((8, 128), f32)
-    k_t = kv[0].reshape(3 * TOK, HD).T
+    far_k_t = kv[0, FAR].T
     for hs in HEAD_SETS:
-        g = dot_nn(k_t, ds[:, span(hs)]) * norm[hs]
+        f, inv = stats[hs]
+        g = dot_nn(far_k_t, ds[rows(FAR), span(hs)])
+        g = (gq_t[:, span(hs)] * f + g) * (inv * SCALE)
         square = square + fold(g * g)
         for i, h in enumerate(hs):
             gq[:, h * HD : (h + 1) * HD] = g[:, i * TOK : (i + 1) * TOK].T.astype(bf16)
-
     outs = [pltpu.make_async_copy(gq, gq_hbm, out_sem.at[0])]
     outs[0].start()
 
-    for side in (NEAR, FAR):
-        for c in returns[side]:
-            c.wait_recv()
+    for c in reversed(returns):
+        c.wait_recv()
     for i, dst in ((0, gk_hbm), (1, gv_hbm)):
         g = acc[i, OWN] + back[i, 0].astype(f32) + back[i, 1].astype(f32)
         square = square + fold(g * g)
@@ -285,7 +307,7 @@
     count = TOK * N_CTX * 8 * (GROUP + 2) * HD
     sq_out[0, 0] = jnp.sum(value) / count
 
-    for c in sent + list(sends.values()) + returns[NEAR] + returns[FAR]:
+    for c in sent + list(sends.values()) + returns:
         c.wait_send()
     for c in outs:
         c.wait()
@@ -331,12 +353,13 @@
             pltpu.VMEM((TOK, GROUP * HD), bf16),
             pltpu.VMEM((2, 3, TOK, HD), bf16),
             pltpu.VMEM((3 * TOK, wide), f32),
-            pltpu.VMEM((2 * TOK, wide), bf16),
+            pltpu.VMEM((TOK, wide), bf16),
             pltpu.VMEM((3 * TOK, wide), bf16),
             pltpu.VMEM((3 * TOK, wide), bf16),
             pltpu.VMEM((8, TOK), f32),
             pltpu.VMEM((TOK, TOK), f32),
             pltpu.VMEM((2, 3, TOK, HD), f32),
+            pltpu.VMEM((HD, wide), f32),
             pltpu.VMEM((TOK, GROUP * HD), bf16),
             pltpu.VMEM((2, TOK, HD), bf16),
             pltpu.VMEM((2, 2, TOK, HD), bf16),

time: 56.1 us -> 52.4 us (0.934)
  Pallas kernels: 53.5 us -> 49.9 us
    pallas_call x1, Pallas kernels: 51.5 us -> 47.8 us  [shards(): pl.pallas_call(kernel, out_shape=(jax.ShapeDtypeStruct((TOK, GROUP * HD),...]
where the time goes in v3:
time: 52.4 us; the launch traced here: 52.2 us
  Pallas kernels  49.9 us (95%)
  between operations  2.38 us (5%)
    pallas_call x1, Pallas kernels, shards(): pl.pallas_call(kernel, out_shape=(jax.ShapeDtypeStruct((TOK, GROUP * HD),...  47.8 us
    pallas_call x1, Pallas kernels, shards(): pl.pallas_call(place_outputs, out_shape=tuple((jax.ShapeDtypeStruct(x.sha...  2.01 us

profile of v3, /device:TPU:1, one launch (start us, length us, event | category | flops | bytes accessed | tf_op | source)
XLA Modules:
  0.0 52.2 jit_solution(10067768928410333953)
XLA Ops:
  0.6 47.8 %grads.1 = (bf16[384,896]{1,0:T(8,128)(2,1)}, bf16[384,128]{1,0:T(8,128)(2,1)}, bf16[384,128]{1,0:T(8,128)(2,1)}, f32[1,1]{1,0:T(1,128)}) custom-call(bf16[384,896]{1,0:T(8,128)(2,1)} %q_hbm.1, bf16[384,128]{1,0:T(8,128)(2,1)} %k_hbm.1, bf16[384,128]{1,0:T(8,128)(2,1)} %v_hbm.1, bf16[384,896]{1,0:T(8,128)(2,1)} %do_hbm.1, bf16[384,896]{1,0:T(8,128)(2,1)} %o_hbm.1, ...), custom_call_target="tpu_custom_call" | custom-call | tf_op jit(solution)/shard_map/grads/pallas_call | solution.py:340
  48.5 2.0 %place_outputs.1 = (bf16[384,896]{1,0:T(8,128)(2,1)}, bf16[384,128]{1,0:T(8,128)(2,1)}, bf16[384,128]{1,0:T(8,128)(2,1)}) custom-call(bf16[384,896]{1,0:T(8,128)(2,1)} %get-tuple-element.11.gq, bf16[384,128]{1,0:T(8,128)(2,1)} %get-tuple-element.12.gk, bf16[384,128]{1,0:T(8,128)(2,1)} %get-tuple-element.13.gv), custom_call_target="tpu_custom_call" | custom-call | tf_op jit(solution)/shard_map/place_outputs/pallas_call | solution.py:384

commit v4 on v3

--- a/solution.py
+++ b/solution.py
@@ -39,9 +39,9 @@
 
 
 def kernel(
-    q_hbm, k_hbm, v_hbm, do_hbm, o_hbm, ids,
+    q_hbm, k_hbm, v_hbm, do_hbm, o_hbm, ids_hbm,
     gq_hbm, gk_hbm, gv_hbm, sq_out,
-    q, do, o, kv, s, dpd, p, ds, delta, mask, acc, gq_t, gq, gkv,
+    ids, q, do, o, kv, s, dpd, p, ds, delta, mask, acc, gq_t, gq, gkv,
     part, back, red_a, red_b, red_src,
     load_sem, out_sem, kv_send, kv_recv, part_send, part_recv, red_send, red_recv,
 ):
@@ -57,14 +57,23 @@
     y = lax.rem(hd, 4)
     deep = (hd // 4) * 8 + plane
 
-    def across(j):
-        return {"ctx": plane * 8 + lax.rem(spot + j % 8, 8), "head": hd - y + lax.rem(y + j // 8, 4)}
-
-    def along(j):
-        z = lax.rem(deep + j, 16)
+    x = spot // 2
+
+    def across(dy, dx, dc):
+        there = lax.rem(x + dx, 4) * 2 + (core + dc - 2 * core * dc)
+        return {"ctx": plane * 8 + there, "head": hd - y + lax.rem(y + dy, 4)}
+
+    def along(dz):
+        z = lax.rem(deep + dz, 16)
         return {"ctx": lax.rem(z, 8) * 8 + spot, "head": (z // 8) * 4 + y}
 
-    partners = [[across(j) for j in range(1, 32)], [along(j) for j in range(1, 16)]]
+    def hops(d, n):
+        return min(d, n - d)
+
+    offsets = [(dy, dx, dc) for dy in range(4) for dx in range(4) for dc in range(2)][1:]
+    offsets.sort(key=lambda d: -hops(d[0], 4) - hops(d[1], 4))
+    depths = sorted(range(1, 16), key=lambda d: -hops(d, 16))
+    partners = [[across(*d) for d in offsets], [along(d) for d in depths]]
 
     barrier = pltpu.get_barrier_semaphore()
     greet = [{"ctx": far, "head": hd}, {"ctx": near, "head": hd}] + partners[0] + partners[1]
@@ -73,18 +82,27 @@
     loads = [
         pltpu.make_async_copy(src, dst, load_sem.at[i])
         for i, (src, dst) in enumerate(
-            [(q_hbm, q), (k_hbm, kv.at[0, OWN]), (v_hbm, kv.at[1, OWN]), (do_hbm, do), (o_hbm, o)]
+            [
+                (k_hbm, kv.at[0, OWN]),
+                (v_hbm, kv.at[1, OWN]),
+                (ids_hbm, ids),
+                (do_hbm, do),
+                (o_hbm, o),
+                (q_hbm, q),
+            ]
         )
     ]
     for c in loads:
         c.start()
+    loads[0].wait()
+    loads[1].wait()
     pl.semaphore_wait(barrier, len(greet))
 
     sends = {}
-    for i, src in ((0, k_hbm), (1, v_hbm)):
+    for i in (0, 1):
         for side in (FAR, NEAR):
             c = pltpu.make_async_remote_copy(
-                src_ref=src,
+                src_ref=kv.at[i, OWN],
                 dst_ref=kv.at[i, side],
                 send_sem=kv_send.at[i, side],
                 recv_sem=kv_recv.at[i, side],
@@ -94,6 +112,7 @@
             c.start()
             sends[i, side] = c
 
+    loads[2].wait()
     lane = lax.broadcasted_iota(jnp.int32, (1, TOK), 1)
     row = lax.broadcasted_iota(jnp.int32, (TOK, 1), 0)
     id0, id1 = ids[2 * me], ids[2 * me + 1]
@@ -106,7 +125,7 @@
         for side in (NEAR, FAR)
     }
 
-    for c in loads:
+    for c in loads[3:]:
         c.wait()
 
     cols = lax.broadcasted_iota(jnp.int32, (TOK, HD), 1)
@@ -345,9 +364,10 @@
             jax.ShapeDtypeStruct((TOK, HD), bf16),
             jax.ShapeDtypeStruct((1, 1), f32),
         ),
-        in_specs=[hbm] * 5 + [smem],
+        in_specs=[hbm] * 6,
         out_specs=(hbm, hbm, hbm, smem),
         scratch_shapes=[
+            pltpu.SMEM((2 * N_CTX,), jnp.int32),
             pltpu.VMEM((TOK, GROUP * HD), bf16),
             pltpu.VMEM((TOK, GROUP * HD), bf16),
             pltpu.VMEM((TOK, GROUP * HD), bf16),
@@ -367,7 +387,7 @@
             pltpu.VMEM((32, 1, 128), f32),
             pltpu.VMEM((16, 1, 128), f32),
             pltpu.VMEM((2, 1, 128), f32),
-            dma((5,)),
+            dma((6,)),
             dma((3,)),
             dma((2, 3)),
             dma((2, 3)),

time: 52.4 us -> 51.5 us (0.983)
  Pallas kernels: 49.9 us -> 49 us
    pallas_call x1, Pallas kernels: 47.8 us -> 47 us  [shards(): pl.pallas_call(kernel, out_shape=(jax.ShapeDtypeStruct((TOK, GROUP * HD),...]
where the time goes in v4:
time: 51.5 us; the launch traced here: 51.3 us
  Pallas kernels  49 us (95%)
  between operations  2.38 us (5%)
    pallas_call x1, Pallas kernels, shards(): pl.pallas_call(kernel, out_shape=(jax.ShapeDtypeStruct((TOK, GROUP * HD),...  47 us
    pallas_call x1, Pallas kernels, shards(): pl.pallas_call(place_outputs, out_shape=tuple((jax.ShapeDtypeStruct(x.sha...  2.01 us

profile of v4, /device:TPU:1, one launch (start us, length us, event | category | flops | bytes accessed | tf_op | source)
XLA Modules:
  0.0 51.3 jit_solution(8621230524629659196)
XLA Ops:
  0.6 47.0 %grads.1 = (bf16[384,896]{1,0:T(8,128)(2,1)}, bf16[384,128]{1,0:T(8,128)(2,1)}, bf16[384,128]{1,0:T(8,128)(2,1)}, f32[1,1]{1,0:T(1,128)}) custom-call(bf16[384,896]{1,0:T(8,128)(2,1)} %q_hbm.1, bf16[384,128]{1,0:T(8,128)(2,1)} %k_hbm.1, bf16[384,128]{1,0:T(8,128)(2,1)} %v_hbm.1, bf16[384,896]{1,0:T(8,128)(2,1)} %do_hbm.1, bf16[384,896]{1,0:T(8,128)(2,1)} %o_hbm.1, ...), custom_call_target="tpu_custom_call" | custom-call | tf_op jit(solution)/shard_map/grads/pallas_call | solution.py:359
  47.6 2.0 %place_outputs.1 = (bf16[384,896]{1,0:T(8,128)(2,1)}, bf16[384,128]{1,0:T(8,128)(2,1)}, bf16[384,128]{1,0:T(8,128)(2,1)}) custom-call(bf16[384,896]{1,0:T(8,128)(2,1)} %get-tuple-element.11.gq, bf16[384,128]{1,0:T(8,128)(2,1)} %get-tuple-element.12.gk, bf16[384,128]{1,0:T(8,128)(2,1)} %get-tuple-element.13.gv), custom_call_target="tpu_custom_call" | custom-call | tf_op jit(solution)/shard_map/place_outputs/pallas_call | solution.py:404

commit v5 on v4

--- a/solution.py
+++ b/solution.py
@@ -94,8 +94,140 @@
     ]
     for c in loads:
         c.start()
+    loads[2].wait()
+    lane = lax.broadcasted_iota(jnp.int32, (1, TOK), 1)
+    row = lax.broadcasted_iota(jnp.int32, (TOK, 1), 0)
+    id0, id1 = ids[2 * me], ids[2 * me + 1]
+    qid = jnp.where(lane < BLK, id0, id1)
+    pos_q = qid * BLK + jnp.where(lane < BLK, lane, lane - BLK)
+    pos_k = jnp.where(row < BLK, id0 * BLK + row, id1 * BLK + row - BLK)
+    mask[...] = jnp.where(pos_k <= pos_q, 0.0, NEG).astype(f32)
+    seen = {
+        side: [jnp.where(ids[2 * others[side] + b] < qid, 1, 0) for b in (0, 1)]
+        for side in (NEAR, FAR)
+    }
+
+    for c in loads[3:]:
+        c.wait()
+
+    cols = lax.broadcasted_iota(jnp.int32, (TOK, HD), 1)
+    gather = jnp.zeros((TOK, HD), f32)
+    for h in range(GROUP):
+        c = slice(h * HD, (h + 1) * HD)
+        d = jnp.sum(do[:, c].astype(f32) * o[:, c].astype(f32), axis=1, keepdims=True)
+        gather = jnp.where(cols == h, d, gather)
+    delta[...] = gather.T[:8]
+
+    def stack(ref, hs):
+        return jnp.concatenate([ref[:, h * HD : (h + 1) * HD] for h in hs], axis=0)
+
+    def rep(x, n):
+        return jnp.concatenate([x] * n, axis=1)
+
+    def span(hs):
+        return slice(hs[0] * TOK, (hs[-1] + 1) * TOK)
+
+    def rows(side):
+        return slice(side * TOK, (side + 1) * TOK)
+
+    peaks = {}
+
+    def scores(side, hs):
+        x = dot_nt(kv[0, side], stack(q, hs))
+        if side == OWN:
+            x = x + rep(mask[...], len(hs))
+            peaks[side, hs] = [jnp.max(x, axis=0, keepdims=True)]
+        else:
+            peaks[side, hs] = [
+                jnp.max(x[b * BLK : (b + 1) * BLK], axis=0, keepdims=True) for b in (0, 1)
+            ]
+        s[rows(side), span(hs)] = x
+
+    def dprobs(side, hs):
+        row_delta = jnp.concatenate([delta[h : h + 1] for h in hs], axis=1)
+        return (dot_nt(kv[1, side], stack(do, hs)) - row_delta).astype(bf16)
+
+    def visible(side, b, hs):
+        return rep(seen[side][b], len(hs)) > 0
+
+    def masked_probs(side, hs, m, total):
+        for b in (0, 1):
+            r = slice(side * TOK + b * BLK, side * TOK + (b + 1) * BLK)
+            shift = jnp.where(visible(side, b, hs), m, BIG)
+            e = jnp.exp2((s[r, span(hs)] - shift) * EXP2_SCALE)
+            total = total + jnp.sum(e, axis=0, keepdims=True)
+            p[r, span(hs)] = e.astype(bf16)
+        return total
+
+    def raised(side, hs, m):
+        for b in (0, 1):
+            m = jnp.maximum(m, jnp.where(visible(side, b, hs), peaks[side, hs][b], NEG))
+        return m
+
+    def columns(row, n):
+        return jnp.concatenate(
+            [jnp.broadcast_to(row[:, i * TOK : (i + 1) * TOK], (HD, TOK)).T for i in range(n)],
+            axis=0,
+        )
+
+    def scaled(ref, hs, cols, factor):
+        return (stack(ref, hs).astype(f32) * (cols * factor)).astype(bf16)
+
+    first_stats, stats, far_scale = {}, {}, {}
+
+    def near_part(hs):
+        m = raised(NEAR, hs, peaks[OWN, hs][0])
+        e = jnp.exp2((s[rows(OWN), span(hs)] - m) * EXP2_SCALE)
+        total = jnp.sum(e, axis=0, keepdims=True)
+        w = e.astype(bf16)
+        p[rows(OWN), span(hs)] = w
+        ds[rows(OWN), span(hs)] = dpd[:, span(hs)] * w
+        total = masked_probs(NEAR, hs, m, total)
+        ds[rows(NEAR), span(hs)] = dprobs(NEAR, hs) * p[rows(NEAR), span(hs)]
+        first_stats[hs] = (m, total)
+
+    def far_values(hs, first):
+        m1, total1 = first_stats[hs]
+        m = raised(FAR, hs, m1)
+        f = jnp.exp2((m1 - m) * EXP2_SCALE)
+        total = masked_probs(FAR, hs, m, total1 * f)
+        inv = 1.0 / total
+        stats[hs] = (f, inv)
+        cols = columns(inv, len(hs))
+        far_scale[hs] = cols
+        add(1, FAR, first, dot_nn(p[rows(FAR), span(hs)], scaled(do, hs, cols, 1.0)))
+
+    def add(i, side, first, x):
+        if first:
+            acc[i, side] = x
+        else:
+            acc[i, side] += x
+
+    def far_keys(hs, first):
+        d = dprobs(FAR, hs) * p[rows(FAR), span(hs)]
+        ds[rows(FAR), span(hs)] = d
+        add(0, FAR, first, dot_nn(d, scaled(q, hs, far_scale[hs], SCALE)))
+
+    def send_back(side, i):
+        part[i, side - 1] = acc[i, side].astype(bf16)
+        c = pltpu.make_async_remote_copy(
+            src_ref=part.at[i, side - 1],
+            dst_ref=back.at[i, side - 1],
+            send_sem=part_send.at[i, side - 1],
+            recv_sem=part_recv.at[i, side - 1],
+            device_id={"ctx": others[side], "head": hd},
+            device_id_type=MESH,
+        )
+        c.start()
+        return c
+
+    last = len(HEAD_SETS) - 1
+
     loads[0].wait()
     loads[1].wait()
+    for hs in HEAD_SETS:
+        scores(OWN, hs)
+        dpd[:, span(hs)] = dprobs(OWN, hs)
     pl.semaphore_wait(barrier, len(greet))
 
     sends = {}
@@ -112,138 +244,6 @@
             c.start()
             sends[i, side] = c
 
-    loads[2].wait()
-    lane = lax.broadcasted_iota(jnp.int32, (1, TOK), 1)
-    row = lax.broadcasted_iota(jnp.int32, (TOK, 1), 0)
-    id0, id1 = ids[2 * me], ids[2 * me + 1]
-    qid = jnp.where(lane < BLK, id0, id1)
-    pos_q = qid * BLK + jnp.where(lane < BLK, lane, lane - BLK)
-    pos_k = jnp.where(row < BLK, id0 * BLK + row, id1 * BLK + row - BLK)
-    mask[...] = jnp.where(pos_k <= pos_q, 0.0, NEG).astype(f32)
-    seen = {
-        side: [jnp.where(ids[2 * others[side] + b] < qid, 1, 0) for b in (0, 1)]
-        for side in (NEAR, FAR)
-    }
-
-    for c in loads[3:]:
-        c.wait()
-
-    cols = lax.broadcasted_iota(jnp.int32, (TOK, HD), 1)
-    gather = jnp.zeros((TOK, HD), f32)
-    for h in range(GROUP):
-        c = slice(h * HD, (h + 1) * HD)
-        d = jnp.sum(do[:, c].astype(f32) * o[:, c].astype(f32), axis=1, keepdims=True)
-        gather = jnp.where(cols == h, d, gather)
-    delta[...] = gather.T[:8]
-
-    def stack(ref, hs):
-        return jnp.concatenate([ref[:, h * HD : (h + 1) * HD] for h in hs], axis=0)
-
-    def rep(x, n):
-        return jnp.concatenate([x] * n, axis=1)
-
-    def span(hs):
-        return slice(hs[0] * TOK, (hs[-1] + 1) * TOK)
-
-    def rows(side):
-        return slice(side * TOK, (side + 1) * TOK)
-
-    peaks = {}
-
-    def scores(side, hs):
-        x = dot_nt(kv[0, side], stack(q, hs))
-        if side == OWN:
-            x = x + rep(mask[...], len(hs))
-            peaks[side, hs] = [jnp.max(x, axis=0, keepdims=True)]
-        else:
-            peaks[side, hs] = [
-                jnp.max(x[b * BLK : (b + 1) * BLK], axis=0, keepdims=True) for b in (0, 1)
-            ]
-        s[rows(side), span(hs)] = x
-
-    def dprobs(side, hs):
-        row_delta = jnp.concatenate([delta[h : h + 1] for h in hs], axis=1)
-        return (dot_nt(kv[1, side], stack(do, hs)) - row_delta).astype(bf16)
-
-    def visible(side, b, hs):
-        return rep(seen[side][b], len(hs)) > 0
-
-    def masked_probs(side, hs, m, total):
-        for b in (0, 1):
-            r = slice(side * TOK + b * BLK, side * TOK + (b + 1) * BLK)
-            shift = jnp.where(visible(side, b, hs), m, BIG)
-            e = jnp.exp2((s[r, span(hs)] - shift) * EXP2_SCALE)
-            total = total + jnp.sum(e, axis=0, keepdims=True)
-            p[r, span(hs)] = e.astype(bf16)
-        return total
-
-    def raised(side, hs, m):
-        for b in (0, 1):
-            m = jnp.maximum(m, jnp.where(visible(side, b, hs), peaks[side, hs][b], NEG))
-        return m
-
-    def columns(row, n):
-        return jnp.concatenate(
-            [jnp.broadcast_to(row[:, i * TOK : (i + 1) * TOK], (HD, TOK)).T for i in range(n)],
-            axis=0,
-        )
-
-    def scaled(ref, hs, cols, factor):
-        return (stack(ref, hs).astype(f32) * (cols * factor)).astype(bf16)
-
-    first_stats, stats, far_scale = {}, {}, {}
-
-    def near_part(hs):
-        m = raised(NEAR, hs, peaks[OWN, hs][0])
-        e = jnp.exp2((s[rows(OWN), span(hs)] - m) * EXP2_SCALE)
-        total = jnp.sum(e, axis=0, keepdims=True)
-        w = e.astype(bf16)
-        p[rows(OWN), span(hs)] = w
-        ds[rows(OWN), span(hs)] = dpd[:, span(hs)] * w
-        total = masked_probs(NEAR, hs, m, total)
-        ds[rows(NEAR), span(hs)] = dprobs(NEAR, hs) * p[rows(NEAR), span(hs)]
-        first_stats[hs] = (m, total)
-
-    def far_values(hs, first):
-        m1, total1 = first_stats[hs]
-        m = raised(FAR, hs, m1)
-        f = jnp.exp2((m1 - m) * EXP2_SCALE)
-        total = masked_probs(FAR, hs, m, total1 * f)
-        inv = 1.0 / total
-        stats[hs] = (f, inv)
-        cols = columns(inv, len(hs))
-        far_scale[hs] = cols
-        add(1, FAR, first, dot_nn(p[rows(FAR), span(hs)], scaled(do, hs, cols, 1.0)))
-
-    def add(i, side, first, x):
-        if first:
-            acc[i, side] = x
-        else:
-            acc[i, side] += x
-
-    def far_keys(hs, first):
-        d = dprobs(FAR, hs) * p[rows(FAR), span(hs)]
-        ds[rows(FAR), span(hs)] = d
-        add(0, FAR, first, dot_nn(d, scaled(q, hs, far_scale[hs], SCALE)))
-
-    def send_back(side, i):
-        part[i, side - 1] = acc[i, side].astype(bf16)
-        c = pltpu.make_async_remote_copy(
-            src_ref=part.at[i, side - 1],
-            dst_ref=back.at[i, side - 1],
-            send_sem=part_send.at[i, side - 1],
-            recv_sem=part_recv.at[i, side - 1],
-            device_id={"ctx": others[side], "head": hd},
-            device_id_type=MESH,
-        )
-        c.start()
-        return c
-
-    last = len(HEAD_SETS) - 1
-
-    for hs in HEAD_SETS:
-        scores(OWN, hs)
-        dpd[:, span(hs)] = dprobs(OWN, hs)
     sends[0, NEAR].wait_recv()
     sends[1, NEAR].wait_recv()
     scores(NEAR, HEAD_SETS[0])
@@ -292,9 +292,9 @@
     outs = [pltpu.make_async_copy(gq, gq_hbm, out_sem.at[0])]
     outs[0].start()
 
-    for c in reversed(returns):
-        c.wait_recv()
-    for i, dst in ((0, gk_hbm), (1, gv_hbm)):
+    for i, dst, arrivals in ((1, gv_hbm, (2, 0)), (0, gk_hbm, (3, 1))):
+        for n in arrivals:
+            returns[n].wait_recv()
         g = acc[i, OWN] + back[i, 0].astype(f32) + back[i, 1].astype(f32)
         square = square + fold(g * g)
         gkv[i] = g.astype(bf16)
@@ -302,7 +302,6 @@
         c.start()
         outs.append(c)
 
-    sent = []
     value = jnp.sum(square, axis=0, keepdims=True)
     for r, (place, slots) in enumerate(((y * 8 + spot, red_a), (deep, red_b))):
         red_src[r] = value
@@ -319,17 +318,19 @@
             )
             c.start()
             copies.append(c)
+        if r == 0:
+            for c in list(sends.values()) + returns:
+                c.wait_send()
+        else:
+            for c in outs:
+                c.wait()
         for c in copies:
+            c.wait_send()
+        for c in reversed(copies):
             c.wait_recv()
-        sent += copies
         value = jnp.sum(slots[...], axis=0)
     count = TOK * N_CTX * 8 * (GROUP + 2) * HD
     sq_out[0, 0] = jnp.sum(value) / count
-
-    for c in sent + list(sends.values()) + returns:
-        c.wait_send()
-    for c in outs:
-        c.wait()
 
 
 def place_outputs(gq, gk, gv, gq_out, gk_out, gv_out, wide, narrow, sem_in, sem_out):

time: 51.5 us -> 51.4 us (level)
  no operation moved by 1% of the time
where the time goes in v5:
time: 51.4 us; the launch traced here: 51.2 us
  Pallas kernels  48.8 us (95%)
  between operations  2.38 us (5%)
    pallas_call x1, Pallas kernels, shards(): pl.pallas_call(kernel, out_shape=(jax.ShapeDtypeStruct((TOK, GROUP * HD),...  46.8 us
    pallas_call x1, Pallas kernels, shards(): pl.pallas_call(place_outputs, out_shape=tuple((jax.ShapeDtypeStruct(x.sha...  2.01 us

profile of v5, /device:TPU:1, one launch (start us, length us, event | category | flops | bytes accessed | tf_op | source)
XLA Modules:
  0.0 51.2 jit_solution(1601373623731587164)
XLA Ops:
  0.6 46.8 %grads.1 = (bf16[384,896]{1,0:T(8,128)(2,1)}, bf16[384,128]{1,0:T(8,128)(2,1)}, bf16[384,128]{1,0:T(8,128)(2,1)}, f32[1,1]{1,0:T(1,128)}) custom-call(bf16[384,896]{1,0:T(8,128)(2,1)} %q_hbm.1, bf16[384,128]{1,0:T(8,128)(2,1)} %k_hbm.1, bf16[384,128]{1,0:T(8,128)(2,1)} %v_hbm.1, bf16[384,896]{1,0:T(8,128)(2,1)} %do_hbm.1, bf16[384,896]{1,0:T(8,128)(2,1)} %o_hbm.1, ...), custom_call_target="tpu_custom_call" | custom-call | tf_op jit(solution)/shard_map/grads/pallas_call | solution.py:360
  47.4 2.0 %place_outputs.1 = (bf16[384,896]{1,0:T(8,128)(2,1)}, bf16[384,128]{1,0:T(8,128)(2,1)}, bf16[384,128]{1,0:T(8,128)(2,1)}) custom-call(bf16[384,896]{1,0:T(8,128)(2,1)} %get-tuple-element.11.gq, bf16[384,128]{1,0:T(8,128)(2,1)} %get-tuple-element.12.gk, bf16[384,128]{1,0:T(8,128)(2,1)} %get-tuple-element.13.gv), custom_call_target="tpu_custom_call" | custom-call | tf_op jit(solution)/shard_map/place_outputs/pallas_call | solution.py:405

commit v6 on v5

--- a/solution.py
+++ b/solution.py
@@ -231,8 +231,8 @@
     pl.semaphore_wait(barrier, len(greet))
 
     sends = {}
-    for i in (0, 1):
-        for side in (FAR, NEAR):
+    for side in (FAR, NEAR):
+        for i in (0, 1):
             c = pltpu.make_async_remote_copy(
                 src_ref=kv.at[i, OWN],
                 dst_ref=kv.at[i, side],

time: 51.4 us -> 51.4 us (level)
  no operation moved by 1% of the time
where the time goes in v6:
time: 51.4 us; the launch traced here: 51.2 us
  Pallas kernels  48.8 us (95%)
  between operations  2.38 us (5%)
    pallas_call x1, Pallas kernels, shards(): pl.pallas_call(kernel, out_shape=(jax.ShapeDtypeStruct((TOK, GROUP * HD),...  46.8 us
    pallas_call x1, Pallas kernels, shards(): pl.pallas_call(place_outputs, out_shape=tuple((jax.ShapeDtypeStruct(x.sha...  2.01 us

profile of v6, /device:TPU:1, one launch (start us, length us, event | category | flops | bytes accessed | tf_op | source)
XLA Modules:
  0.0 51.2 jit_solution(6202098353088485060)
XLA Ops:
  0.6 46.8 %grads.1 = (bf16[384,896]{1,0:T(8,128)(2,1)}, bf16[384,128]{1,0:T(8,128)(2,1)}, bf16[384,128]{1,0:T(8,128)(2,1)}, f32[1,1]{1,0:T(1,128)}) custom-call(bf16[384,896]{1,0:T(8,128)(2,1)} %q_hbm.1, bf16[384,128]{1,0:T(8,128)(2,1)} %k_hbm.1, bf16[384,128]{1,0:T(8,128)(2,1)} %v_hbm.1, bf16[384,896]{1,0:T(8,128)(2,1)} %do_hbm.1, bf16[384,896]{1,0:T(8,128)(2,1)} %o_hbm.1, ...), custom_call_target="tpu_custom_call" | custom-call | tf_op jit(solution)/shard_map/grads/pallas_call | solution.py:360
  47.4 2.0 %place_outputs.1 = (bf16[384,896]{1,0:T(8,128)(2,1)}, bf16[384,128]{1,0:T(8,128)(2,1)}, bf16[384,128]{1,0:T(8,128)(2,1)}) custom-call(bf16[384,896]{1,0:T(8,128)(2,1)} %get-tuple-element.11.gq, bf16[384,128]{1,0:T(8,128)(2,1)} %get-tuple-element.12.gk, bf16[384,128]{1,0:T(8,128)(2,1)} %get-tuple-element.13.gv), custom_call_target="tpu_custom_call" | custom-call | tf_op jit(solution)/shard_map/place_outputs/pallas_call | solution.py:405
